TPU v7x, 256 devices: a whole 4x4x8 slice. The times are simulated.
256 devices in a mesh: pool: 32 (over y, x, core), tp: 8 (over z).
Axes of the slice: x: 4, y: 4, z: 8, core: 2. Of those that a mesh axis runs over, the one named last changes fastest.
Arguments:
- hidden: bfloat16 [1024, 8192], P('pool', 'tp'), may hold values from -6 to 6
- queries: bfloat16 [1024, 8192], P('pool', 'tp'), may hold values from -6 to 6
- key_value_weight: bfloat16 [8192, 8, 256], P('tp'), may hold values from -0.0625 to 0.0625
- adapter_down_maps: bfloat16 [256, 8192, 128], P('pool', 'tp'), may hold values from -0.0625 to 0.0625
- adapter_up_maps: bfloat16 [256, 2, 64, 8, 128], P('pool', None, None, 'tp'), may hold values from -0.75 to 0.75
- key_value_pages: bfloat16 [8704, 16, 8, 256], P('pool', None, 'tp'), may hold values from -6 to 6
- row_adapter_index: int32 [1024], P('pool'), may hold values from 0 to 255, as said below
- adapter_page_position: int32 [256], replicated, may hold values from 0 to 255, as said below
- row_page_table: int32 [1024, 16], P('pool'), may hold values from 0 to 271, as said below
- cached_length: int32 [1024], P('pool'), may hold values from 1 to 256, as said below
Outputs:
- new_kv: bfloat16 [1024, 8, 256], P('pool', 'tp')
- attended: bfloat16 [1024, 8192], P('pool', 'tp')
Inputs may be any that keep to these rules, and one draw needn't show every extreme that they name: `row_adapter_index`: of the rows of one pool device, at most 2 use adapters whose pages stand on any one pool device; on one pool device stand the adapters of exactly 2 rows of every device. `adapter_page_position`: a permutation; adapter a's pages stand on pool device adapter_page_position[a] // 8, at local index adapter_page_position[a] % 8. `row_page_table`: entries are pages of the row's own pool device; row r's cached position p lies in entry p // 16; the pages used by the rows of one device are distinct and number exactly 272; entries past a row's length are arbitrary pages. `cached_length`: every pool device has a row of exactly 256 positions.
All inputs are finite; a program needn't handle non-finite values.
Results may differ from a plain program's by a relative error of at most 0.0055.
Values may be sent and summed in bfloat16 or wider, within the bound.
A program may use at most 128 MiB of HBM per device.

v0:
```python
import math

import jax
import jax.numpy as jnp
from jax import lax
from jax.sharding import PartitionSpec as P

adapter_scale = 0.5


def body(
    hidden,
    queries,
    key_value_weight,
    adapter_down_maps,
    adapter_up_maps,
    key_value_pages,
    row_adapter_index,
    adapter_page_position,
    row_page_table,
    cached_length,
):
    row_count = hidden.shape[0]
    feature_share = hidden.shape[1]
    key_value_share = key_value_pages.shape[2]
    head_width = key_value_pages.shape[3] // 2
    double_rank = adapter_down_maps.shape[2]
    rank_width = double_rank // 2
    adapter_total = adapter_down_maps.shape[0]
    pool_width = lax.axis_size("pool")
    page_capacity = max(2, 2 * row_count // pool_width)
    slot_total = pool_width * page_capacity
    base_kv = lax.psum_scatter(
        jnp.einsum("rd,dhc->hrc", hidden, key_value_weight, preferred_element_type=jnp.float32),
        "tp",
        scatter_dimension=0,
        tiled=True,
    )
    base_kv = jnp.transpose(base_kv, (1, 0, 2))
    table_hit = (
        row_adapter_index[:, None]
        == jnp.arange(adapter_page_position.shape[0], dtype=jnp.int32)[None, :]
    )
    position = jnp.sum(jnp.where(table_hit, adapter_page_position[None, :], 0), axis=1)
    owner_of = position // adapter_total
    local_page = position % adapter_total
    same_owner = owner_of[:, None] == owner_of[None, :]
    row_order = jnp.arange(row_count, dtype=jnp.int32)
    earlier = row_order[None, :] < row_order[:, None]
    slot_rank = jnp.sum(same_owner & earlier, axis=1)
    target = owner_of * page_capacity + slot_rank
    placing = target[None, :] == jnp.arange(slot_total, dtype=jnp.int32)[:, None]
    place_mask = placing.astype(jnp.bfloat16)
    send_x = jnp.dot(place_mask, hidden, preferred_element_type=jnp.float32).astype(jnp.bfloat16)
    send_local = jnp.sum(jnp.where(placing, local_page[None, :], 0), axis=1)
    wanted = lax.all_to_all(
        send_local.reshape(pool_width, page_capacity),
        "pool",
        split_axis=0,
        concat_axis=0,
        tiled=True,
    )
    flat_requested = wanted.reshape(slot_total)
    down_map_selected = adapter_down_maps[flat_requested].reshape(
        pool_width, page_capacity, feature_share, double_rank
    )
    up_map_selected = adapter_up_maps[flat_requested].reshape(
        pool_width, page_capacity, 2, rank_width, key_value_share, head_width
    )
    got_down, got_up = (
        lax.all_to_all(down_map_selected, "pool", split_axis=0, concat_axis=0, tiled=True),
        lax.all_to_all(up_map_selected, "pool", split_axis=0, concat_axis=0, tiled=True),
    )
    partial_rank = jnp.einsum(
        "sd,sdk->sk",
        send_x,
        got_down.reshape(slot_total, feature_share, double_rank),
        preferred_element_type=jnp.float32,
    )
    shrink = lax.psum(partial_rank, "tp").astype(jnp.bfloat16)
    up_slots = got_up.reshape(slot_total, 2, rank_width, key_value_share, head_width)
    key_value_halves = []
    for member in range(2):
        key_value_halves.append(
            jnp.einsum(
                "sr,srhd->shd",
                shrink[:, member * rank_width : (member + 1) * rank_width],
                up_slots[:, member],
                preferred_element_type=jnp.float32,
            )
        )
    delta_slots = (
        (jnp.concatenate(key_value_halves, axis=2) * adapter_scale)
        .astype(jnp.bfloat16)
        .reshape(slot_total, key_value_share * 2 * head_width)
    )
    delta_rows = jnp.dot(place_mask.T, delta_slots, preferred_element_type=jnp.float32).reshape(
        row_count, key_value_share, 2 * head_width
    )
    new_kv = (base_kv + delta_rows).astype(jnp.bfloat16)
    gathered = key_value_pages[row_page_table]
    cache_span = gathered.shape[1] * gathered.shape[2]
    gathered = gathered.reshape(row_count, cache_span, key_value_share, 2 * head_width)
    group_size = queries.shape[1] // (key_value_share * head_width)
    query_heads = queries.reshape(row_count, key_value_share, group_size, head_width)
    score_scale = 1.0 / math.sqrt(head_width)
    cache_scores = (
        jnp.einsum(
            "rkgd,rpkd->rkgp",
            query_heads,
            gathered[..., :head_width],
            preferred_element_type=jnp.float32,
        )
        * score_scale
    )
    own_score = (
        jnp.einsum(
            "rkgd,rkd->rkg",
            query_heads,
            new_kv[..., :head_width],
            preferred_element_type=jnp.float32,
        )
        * score_scale
    )
    is_valid = (jnp.arange(cache_span, dtype=jnp.int32)[None, :] < cached_length[:, None])[
        :, None, None, :
    ]
    row_max = jnp.maximum(jnp.max(jnp.where(is_valid, cache_scores, -jnp.inf), axis=3), own_score)
    cache_weight = jnp.where(is_valid, jnp.exp(cache_scores - row_max[..., None]), 0.0)
    own_weight = jnp.exp(own_score - row_max)
    weight_sum = jnp.sum(cache_weight, axis=3) + own_weight
    own_rounded = lax.optimization_barrier(own_weight.astype(jnp.bfloat16)).astype(jnp.float32)
    blended = jnp.einsum(
        "rkgp,rpkd->rkgd",
        cache_weight.astype(jnp.bfloat16),
        gathered[..., head_width:],
        preferred_element_type=jnp.float32,
    )
    blended = blended + own_rounded[..., None] * new_kv[:, :, None, head_width:].astype(jnp.float32)
    attended = (
        (blended / weight_sum[..., None])
        .astype(jnp.bfloat16)
        .reshape(row_count, key_value_share * group_size * head_width)
    )
    return (new_kv, attended)


def solution(mesh):
    placed = (
        P("pool", "tp"),
        P("pool", "tp"),
        P("tp", None, None),
        P("pool", "tp", None),
        P("pool", None, None, "tp", None),
        P("pool", None, "tp", None),
        P("pool"),
        P(),
        P("pool", None),
        P("pool"),
    )
    return jax.shard_map(
        body,
        mesh=mesh,
        in_specs=placed,
        out_specs=(P("pool", "tp", None), P("pool", "tp")),
        check_vma=False,
    )
```

profile of v0, /device:TPU:1, one launch (start us, length us, event | category | flops | bytes accessed | tf_op | source)
XLA Modules:
  0.0 312.3 jit_solution(13354511981084425566)
XLA Ops:
  7.2 0.0 copy-start
  7.2 1.0 select_reduce_fusion.1
  8.2 0.2 convert_reduce_fusion
  8.4 0.1 select_reduce_fusion.2
  8.5 0.1 all_to_all.12
  8.6 15.3 %all_to_all.19 = s32[32,1,2]{2,1,0:T(1,128)S(1)} all-to-all(s32[32,1,2]{2,1,0:T(1,128)S(1)} %bitcast.96), channel_id=1, replica_groups=mesh['pool'=32,'tp'=8] {'pool'}, dimensions={0} | all-to-all | bytes 512 | tf_op jit(solution)/shard_map/all_to_all | solution.py:56
  23.9 0.5 broadcast.193
  24.4 0.7 reduce.8
  25.1 0.1 reshape.228
  25.3 9.0 %gather_fusion = bf16[64,1024,128]{2,1,0:T(8,128)(2,1)} fusion(bf16[8,1024,128]{2,1,0:T(8,128)(2,1)} %param.13, s32[1024]{0:T(1024)S(1)} %pad_clamp_fusion.1), kind=kCustom, calls=%fused_computation | custom fusion | bytes 33554688 | tf_op jit(solution)/shard_map/gather | solution.py:64
  34.2 0.0 copy-start.2
  34.2 5.6 %all-to-all-start.1 = ((bf16[32,2,1024,128]{3,2,1,0:T(8,128)(2,1)}), bf16[32,2,1024,128]{3,2,1,0:T(8,128)(2,1)}, u32[]{:S(2)}, u32[]{:S(2)}) async-start(bf16[32,2,1024,128]{3,2,1,0:T(8,128)(2,1)} %bitcast.83), calls=%async_computation.2 | async-start | bytes 33554432 | tf_op jit(solution)/shard_map/all_to_all | solution.py:71
  39.8 0.0 copy-start.1
  39.8 0.0 reduce-scatter.2.cloned.1.call-start
  39.9 0.0 copy-done.2
  39.9 3.7 %fusion.5 = f32[8,32,256]{2,1,0:T(8,128)} fusion(bf16[1024,8,256]{2,1,0:T(8,128)(2,1)} %param.12, bf16[32,1024]{1,0:T(8,128)(2,1)S(1)} %copy-done.2), kind=kOutput, calls=%fused_computation.10 | convolution fusion | flops 134217728 | bytes 4521984 | tf_op jit(solution)/shard_map/rd,dhc->hrc/dot_general | solution.py:34
  43.6 0.0 reduce-scatter.2.cloned.1.call-update
  43.6 0.0 copy-done.1
  43.7 0.0 copy-start.5
  43.7 0.0 copy-start.4
  43.7 2.1 gather_fusion.1
  45.8 195.5 %all-to-all-done.1 = bf16[32,2,1024,128]{3,2,1,0:T(8,128)(2,1)} async-done(((bf16[32,2,1024,128]{3,2,1,0:T(8,128)(2,1)}), bf16[32,2,1024,128]{3,2,1,0:T(8,128)(2,1)}, u32[]{:S(2)}, u32[]{:S(2)}) %all-to-all-start.1) | async-done | bytes 16777248 | tf_op jit(solution)/shard_map/all_to_all | solution.py:71
  241.3 16.5 %all-to-all-start.2 = ((bf16[32,2,2,64,1,128]{5,3,2,1,4,0:T(8,128)(2,1)}), bf16[32,2,2,64,1,128]{5,3,2,1,4,0:T(8,128)(2,1)}, u32[]{:S(2)}, u32[]{:S(2)}) async-start(bf16[32,2,2,64,1,128]{5,3,2,1,4,0:T(8,128)(2,1)} %bitcast.85), calls=%async_computation.3 | async-start | bytes 4194304 | tf_op jit(solution)/shard_map/all_to_all | solution.py:72
  257.8 0.0 copy-done.5
  257.8 0.0 copy-done.4
  257.9 0.1 copy.20
  258.0 0.1 reshape.265
  258.0 0.0 copy-done
  258.1 0.0 copy-start.6
  258.1 3.4 %gather_fusion.2 = bf16[512,16,256]{2,1,0:T(8,128)(2,1)} fusion(bf16[272,16,256]{2,1,0:T(8,128)(2,1)S(1)} %bitcast.82, s32[1024]{0:T(1024)S(1)} %pad_clamp_fusion), kind=kCustom, calls=%fused_computation.2 | custom fusion | bytes 8390656 | tf_op jit(solution)/shard_map/gather | solution.py:101
  261.5 0.3 fusion.8
  261.8 0.0 copy-done.6
  261.8 0.1 iota_compare_fusion
  261.9 2.3 select_reduce_fusion
  264.2 7.0 %fusion.16 = f32[64,1,128]{2,1,0:T(1,128)S(1)} fusion(bf16[64,1024,128]{2,1,0:T(8,128)(2,1)} %bitcast.7, bf16[64,1024,1]{1,0,2:T(8,128)(2,1)S(1)} %fusion.8), kind=kOutput, calls=%fused_computation.25 | convolution fusion | flops 16777216 | bytes 16941056 | tf_op jit(solution)/shard_map/sd,sdk->sk/dot_general | solution.py:74
  271.2 26.9 %psum.7 = bf16[64,128]{1,0:T(8,128)(2,1)S(1)} all-reduce(f32[64,128]{1,0:T(8,128)S(1)} %bitcast.88), channel_id=1, replica_groups=mesh['pool'=32,'tp'=8] {'tp'}, use_global_device_ids=true, to_apply=%region_4.5 | all-reduce | flops 8192 | bytes 49152 | tf_op jit(solution)/shard_map/psum | solution.py:80
  298.1 0.1 slice_bitcast_fusion.17
  298.2 0.0 all-to-all-done.2
  298.2 1.6 fusion.15
  299.8 1.6 fusion.14
  301.4 0.0 reduce-scatter.2.cloned.1.call-done
  301.4 1.0 fusion.13
  302.4 0.0 copy-start.3
  302.4 0.1 fusion.27
  302.6 0.2 bitcast_reduce_fusion
  302.8 2.0 fusion.11
  304.8 0.7 copy.44
  305.5 0.0 copy-done.3
  (11 shorter events, 0.1 us)
Async XLA Ops:
  7.2 250.9 %copy-start = (bf16[272,16,1,256]{3,1,2,0:T(8,128)(2,1)S(1)}, bf16[272,16,1,256]{3,1,2,0:T(8,128)(2,1)}, u32[]{:S(2)}) copy-start(bf16[272,16,1,256]{3,1,2,0:T(8,128)(2,1)} %param.15) | copy-start | bytes 6684676
  34.2 5.6 %copy-start.2 = (bf16[32,1024]{1,0:T(8,128)(2,1)S(1)}, bf16[32,1024]{1,0:T(8,128)(2,1)}, u32[]{:S(2)}) copy-start(bf16[32,1024]{1,0:T(8,128)(2,1)} %param.10) | copy-start | bytes 196612
  34.2 207.1 %all-to-all-start.1 = ((bf16[32,2,1024,128]{3,2,1,0:T(8,128)(2,1)}), bf16[32,2,1024,128]{3,2,1,0:T(8,128)(2,1)}, u32[]{:S(2)}, u32[]{:S(2)}) async-start(bf16[32,2,1024,128]{3,2,1,0:T(8,128)(2,1)} %bitcast.83), calls=%async_computation.2 | async-start | bytes 33554432 | tf_op jit(solution)/shard_map/all_to_all | solution.py:71
  39.8 3.8 %copy-start.1 = (bf16[8,2,64,1,128]{4,2,3,1,0:T(8,128)(2,1)S(1)}, bf16[8,2,64,1,128]{4,2,3,1,0:T(8,128)(2,1)}, u32[]{:S(2)}) copy-start(bf16[8,2,64,1,128]{4,2,3,1,0:T(8,128)(2,1)} %param.14) | copy-start | bytes 786436
  39.8 261.6 %reduce-scatter.2.cloned.1.call-start = ((), (), s32[]{:S(2)}) async-start(), calls=%async_computation.4 | async-start | bytes 294912 | tf_op jit(solution)/shard_map/reduce_scatter | solution.py:33
  43.7 214.2 %copy-start.5 = (s32[32,16]{0,1:T(8,128)S(1)}, s32[32,16]{0,1:T(8,128)}, u32[]{:S(2)}) copy-start(s32[32,16]{0,1:T(8,128)} %param.18) | copy-start | bytes 6148
  43.7 214.2 %copy-start.4 = (bf16[32,1024]{1,0:T(8,128)(2,1)S(1)}, bf16[32,1024]{1,0:T(8,128)(2,1)}, u32[]{:S(2)}) copy-start(bf16[32,1024]{1,0:T(8,128)(2,1)} %param.11) | copy-start | bytes 196612
  241.3 56.9 %all-to-all-start.2 = ((bf16[32,2,2,64,1,128]{5,3,2,1,4,0:T(8,128)(2,1)}), bf16[32,2,2,64,1,128]{5,3,2,1,4,0:T(8,128)(2,1)}, u32[]{:S(2)}, u32[]{:S(2)}) async-start(bf16[32,2,2,64,1,128]{5,3,2,1,4,0:T(8,128)(2,1)} %bitcast.85), calls=%async_computation.3 | async-start | bytes 4194304 | tf_op jit(solution)/shard_map/all_to_all | solution.py:72
  258.1 3.7 %copy-start.6 = (s32[32]{0:T(128)S(1)}, s32[32]{0:T(128)}, u32[]{:S(2)}) copy-start(s32[32]{0:T(128)} %param.19) | copy-start | bytes 388
  302.4 3.1 copy-start.3
Sparse Core Ops, SparseCore 0:
  43.8 35.7 reduce-scatter.1
where the time goes:
time: 318 us; the launch traced here: 312 us
  waiting for transfers between devices  196 us (62%)
  blocking collectives  42.2 us (13%)
  starting transfers between devices  22.1 us (7%)
  matrix products  19.7 us (6%)
  local copies, waits for them, and re-layouts  16.2 us (5%)
  between operations  14.3 us (4%)
    all_to_all x1, waiting for transfers between devices, body(): lax.all_to_all(down_map_selected, 'pool', split_axis=0, concat_axis=0, ti...  196 us
    psum x1, blocking collectives, body(): shrink = lax.psum(partial_rank, 'tp').astype(jnp.bfloat16)  26.9 us
    all_to_all x1, starting transfers between devices, body(): lax.all_to_all(up_map_selected, 'pool', split_axis=0, concat_axis=0, tile...  16.5 us
    all_to_all x1, blocking collectives, body(): lax.all_to_all(send_local.reshape(pool_width, page_capacity), 'pool', spl...  15.3 us
    gather x1, local copies, waits for them, and re-layouts, body(): adapter_down_maps[flat_requested]  8.95 us
    dot_general x1, matrix products, body(): jnp.einsum('sd,sdk->sk', send_x, got_down.reshape(slot_total, feature_sha...  7 us
  transfers between devices with their start and end apart: 3, of which 1 were waited for; matrix products, arithmetic and copies ran while one was open for 7% of the time, Pallas kernels for 0%

commit v1 on v0

v1 whole, which is shorter than its diff:
```python
import functools
import math

import jax
import jax.numpy as jnp
from jax import lax
from jax.experimental import pallas as pl
from jax.experimental.pallas import tpu as pltpu
from jax.sharding import PartitionSpec as P

adapter_scale = 0.5
MESH = pl.DeviceIdType.MESH
LANES = 128
CAP = 2
NEG = -1e30
F32 = jnp.float32
BF16 = jnp.bfloat16


def iota(shape, dim):
    return lax.broadcasted_iota(jnp.int32, shape, dim)


def ring(extent, step):
    return min(step, extent - step)


def pool_offsets(dims):
    ny, nx, nc = dims
    steps = [(a, b, c) for a in range(ny) for b in range(nx) for c in range(nc)][1:]
    return sorted(steps, key=lambda s: -(ring(ny, s[0]) + ring(nx, s[1])) * 2 - s[2])


def pool_partner(me, dims, step):
    ny, nx, nc = dims
    y = lax.rem(me // (nx * nc) + step[0], ny)
    x = lax.rem(lax.rem(me // nc, nx) + step[1], nx)
    c = lax.rem(lax.rem(me, nc) + step[2], nc)
    return (y * nx + x) * nc + c


def kernel(
    dims,
    heads,
    hid_hbm,
    q_hbm,
    w_hbm,
    down_hbm,
    up_hbm,
    pages_hbm,
    rai_hbm,
    app_hbm,
    table_hbm,
    length_hbm,
    new_kv_ref,
    attended_ref,
    hid,
    q,
    w,
    down,
    up,
    pages,
    rai,
    app,
    table,
    length,
    send_rows,
    recv_rows,
    row_f32,
    meta_f32,
    send_base,
    recv_base,
    send_rank,
    recv_rank,
    send_delta,
    recv_delta,
    bias,
    scores,
    load_sem,
    row_send_sem,
    row_recv_sem,
    base_send_sem,
    base_recv_sem,
    rank_send_sem,
    rank_recv_sem,
    delta_send_sem,
    delta_recv_sem,
):
    me = lax.axis_index("pool")
    tp = lax.axis_index("tp")
    n_pool = dims[0] * dims[1] * dims[2]
    n_tp = heads
    rows, feats = hid.shape
    chunks = feats // LANES
    adapters = down.shape[0] // feats
    head = LANES
    group = q.shape[1] // head
    slots = CAP * n_pool
    span = CAP * chunks
    offsets = pool_offsets(dims)
    partners = [pool_partner(me, dims, s) for s in offsets]
    tp_partners = [lax.rem(tp + s, n_tp) for s in range(1, n_tp)]

    loads = [
        pltpu.make_async_copy(src, dst, load_sem.at[i])
        for i, (src, dst) in enumerate(
            (
                (rai_hbm, rai),
                (app_hbm, app),
                (hid_hbm, hid),
                (w_hbm, w),
                (table_hbm, table),
                (length_hbm, length),
                (q_hbm, q),
                (down_hbm, down),
                (pages_hbm, pages),
                (up_hbm, up),
            )
        )
    ]
    (l_rai, l_app, l_hid, l_w, l_table, l_length, l_q, l_down, l_pages, l_up) = loads
    for load in loads:
        load.start()

    barrier = pltpu.get_barrier_semaphore()
    for p in partners:
        pl.semaphore_signal(barrier, inc=1, device_id=(p, tp), device_id_type=MESH)
    for t in tp_partners:
        pl.semaphore_signal(barrier, inc=1, device_id=(me, t), device_id_type=MESH)

    l_rai.wait()
    l_app.wait()
    eye = iota((rows, rows), 0) == iota((rows, rows), 1)
    rai_row = rai[...].astype(F32)
    rai_col = jnp.sum(jnp.where(eye, rai_row, 0.0), axis=1, keepdims=True)
    n_adapters = app.shape[1]
    hit = rai_col == iota((rows, n_adapters), 1).astype(F32)
    position = jnp.sum(jnp.where(hit, app[...].astype(F32), 0.0), axis=1, keepdims=True)
    owner = jnp.floor(position * (1.0 / adapters))
    local = position - owner * adapters
    owner_row = jnp.sum(jnp.where(eye, owner, 0.0), axis=0, keepdims=True)
    earlier = iota((rows, rows), 1) < iota((rows, rows), 0)
    rank = jnp.sum(jnp.where((owner == owner_row) & earlier, 1.0, 0.0), axis=1, keepdims=True)
    target = owner * CAP + rank

    lanes = chunks * rows
    lane_eye = iota((rows, lanes), 0) == lax.rem(iota((rows, lanes), 1), rows)
    target_lane = jnp.sum(jnp.where(lane_eye, target, 0.0), axis=0, keepdims=True)
    line = iota((slots * chunks, lanes), 0)
    place = ((line // chunks).astype(F32) == target_lane) & (
        lax.rem(line, chunks) == iota((slots * chunks, lanes), 1) // rows
    )
    place = jnp.where(place, 1.0, 0.0).astype(BF16)
    l_hid.wait()
    stacked = jnp.concatenate([hid[:, c * LANES : (c + 1) * LANES] for c in range(chunks)], axis=0)
    local_lines = jnp.broadcast_to(local, (rows, LANES)).astype(BF16)
    local_stack = jnp.concatenate([local_lines] * chunks, axis=0)
    packets = jnp.dot(
        place, jnp.concatenate([stacked, local_stack], axis=1), preferred_element_type=F32
    ).astype(BF16)
    send_rows[:, 0:span, :] = packets[:, :LANES].reshape(n_pool, span, LANES)
    send_rows[:, span : 2 * span, :] = packets[:, LANES:].reshape(n_pool, span, LANES)

    pl.semaphore_wait(barrier, len(partners) + len(tp_partners))

    row_copies = []
    for k, p in enumerate(partners):
        copy = pltpu.make_async_remote_copy(
            src_ref=send_rows.at[p],
            dst_ref=recv_rows.at[me],
            send_sem=row_send_sem.at[k],
            recv_sem=row_recv_sem.at[k],
            device_id=(p, tp),
            device_id_type=MESH,
        )
        copy.start()
        row_copies.append(copy)
    recv_rows[me] = send_rows[me]

    wide = LANES * heads
    spread = iota((LANES, wide), 0) == iota((LANES, wide), 1) // heads
    spread = jnp.where(spread, 1.0, 0.0).astype(BF16)
    repeated = jnp.dot(stacked, spread, preferred_element_type=F32).astype(BF16)
    head_of_lane = lax.rem(iota((rows, wide), 1), heads)
    l_w.wait()
    base = jnp.zeros((heads * rows, 2 * head), F32)
    for c in range(chunks):
        piece = repeated[c * rows : (c + 1) * rows, :]
        masked = jnp.concatenate(
            [jnp.where(head_of_lane == g, piece, jnp.zeros_like(piece)) for g in range(heads)], axis=0
        )
        base += jnp.dot(masked, w[c * wide : (c + 1) * wide, :], preferred_element_type=F32)
    send_base[...] = base.astype(BF16).reshape(heads, rows, 2 * head)
    base_copies = []
    for k, t in enumerate(tp_partners):
        copy = pltpu.make_async_remote_copy(
            src_ref=send_base.at[t],
            dst_ref=recv_base.at[tp],
            send_sem=base_send_sem.at[k],
            recv_sem=base_recv_sem.at[k],
            device_id=(me, t),
            device_id_type=MESH,
        )
        copy.start()
        base_copies.append(copy)
    recv_base[tp] = send_base[tp]

    l_down.wait()
    for copy in row_copies:
        copy.wait_recv()
    row_f32[...] = recv_rows[:, 0:span, :].astype(F32).reshape(n_pool * span, LANES)
    meta_f32[...] = recv_rows[:, span : 2 * span, :].astype(F32).reshape(n_pool * span, LANES)
    taken = jnp.concatenate(
        [
            jnp.concatenate(
                [row_f32[pl.ds(s * chunks + c, n_pool, stride=span), :] for c in range(chunks)], axis=1
            )
            for s in range(CAP)
        ],
        axis=0,
    ).astype(BF16)
    adapter_of = jnp.concatenate(
        [meta_f32[pl.ds(s * chunks, n_pool, stride=span), :] for s in range(CAP)], axis=0
    )
    partial = jnp.zeros((slots, LANES), F32)
    for a in range(adapters):
        product = jnp.dot(taken, down[a * feats : (a + 1) * feats, :], preferred_element_type=F32)
        partial = jnp.where(adapter_of == float(a), product, partial)
    send_rank[...] = partial.astype(BF16)
    rank_copies = []
    for k, t in enumerate(tp_partners):
        copy = pltpu.make_async_remote_copy(
            src_ref=send_rank,
            dst_ref=recv_rank.at[tp],
            send_sem=rank_send_sem.at[k],
            recv_sem=rank_recv_sem.at[k],
            device_id=(me, t),
            device_id_type=MESH,
        )
        copy.start()
        rank_copies.append(copy)
    recv_rank[tp] = send_rank[...]

    l_table.wait()
    l_length.wait()
    entries, _ = table.shape
    positions = pages.shape[0]
    page = 16
    eye_bf16 = jnp.where(eye, 1.0, 0.0).astype(BF16)
    entry = table[...]
    high, low = entry // 16, lax.rem(entry, 16)
    turn = (((1,), (1,)), ((), ()))
    table_rows = (
        lax.dot_general(eye_bf16, high.astype(F32).astype(BF16), turn, preferred_element_type=F32) * 16.0
        + lax.dot_general(eye_bf16, low.astype(F32).astype(BF16), turn, preferred_element_type=F32)
    )
    length_col = jnp.sum(jnp.where(eye, length[...].astype(F32), 0.0), axis=1, keepdims=True)
    page_blocks = pl.cdiv(positions // page, LANES)
    page_id = iota((rows, page_blocks * LANES), 1).astype(F32)
    held = jnp.zeros((rows, page_blocks * LANES), F32)
    for j in range(entries):
        valid = jnp.clip(length_col - float(page * j), 0.0, float(page))
        held += jnp.where(table_rows[:, j : j + 1] == page_id, valid, 0.0)
    held = held.astype(BF16)
    widen = iota((LANES, LANES * page), 0) == iota((LANES, LANES * page), 1) // page
    widen = jnp.where(widen, 1.0, 0.0).astype(BF16)
    for b in range(page_blocks):
        first = b * LANES * page
        width = min(LANES * page, positions - first)
        count = jnp.dot(held[:, b * LANES : (b + 1) * LANES], widen[:, :width], preferred_element_type=F32)
        within = lax.rem(iota((rows, width), 1), page).astype(F32)
        bias[:, first : first + width] = jnp.where(within < count, 0.0, NEG)

    l_q.wait()
    l_pages.wait()
    query = jnp.concatenate([q[:, h * head : (h + 1) * head] for h in range(group)], axis=0)
    scale = math.log2(math.e) / math.sqrt(head)
    tile = 256
    tiles = positions // tile
    pairs = group * rows

    def score_step(j, largest):
        at = pl.ds(pl.multiple_of(j * tile, tile), tile)
        s = lax.dot_general(query, pages[at, 0:head], turn, preferred_element_type=F32) * scale
        s = (s.reshape(group, rows, tile) + bias[:, at][None]).reshape(pairs, tile)
        scores[j] = s
        return jnp.maximum(largest, jnp.maximum(s[:, :LANES], s[:, LANES:]))

    largest = lax.fori_loop(0, tiles, score_step, jnp.full((pairs, LANES), NEG, F32))
    largest = jnp.max(largest, axis=1, keepdims=True)

    def weight_step(j, carry):
        total, blended = carry
        at = pl.ds(pl.multiple_of(j * tile, tile), tile)
        weight = jnp.exp2(scores[j] - largest)
        total = total + weight[:, :LANES] + weight[:, LANES:]
        blended = blended + jnp.dot(
            weight.astype(BF16), pages[at, head : 2 * head], preferred_element_type=F32
        )
        return total, blended

    l_up.wait()
    for copy in rank_copies:
        copy.wait_recv()
    shrink = recv_rank[0].astype(F32)
    for t in range(1, n_tp):
        shrink += recv_rank[t].astype(F32)
    shrink = shrink.astype(BF16).astype(F32)
    key_lane = iota((slots, LANES), 1) < LANES // 2
    halves = [
        jnp.concatenate(
            [jnp.where((adapter_of == float(a)) & lane, shrink, 0.0) for a in range(adapters)], axis=1
        )
        for lane in (key_lane, jnp.logical_not(key_lane))
    ]
    delta = jnp.dot(jnp.concatenate(halves, axis=0).astype(BF16), up[...], preferred_element_type=F32)
    delta = (delta * adapter_scale).astype(BF16).astype(F32)
    for s in range(CAP):
        for half in range(2):
            first = half * slots + s * n_pool
            send_delta[pl.ds(s * 2 + half, n_pool, stride=8), :] = delta[first : first + n_pool, :]
    for blank in range(2 * CAP, 8):
        send_delta[pl.ds(blank, n_pool, stride=8), :] = jnp.zeros((n_pool, LANES), F32)
    delta_copies = []
    mine = pl.ds(pl.multiple_of(me * 8, 8), 8)
    for k, p in enumerate(partners):
        copy = pltpu.make_async_remote_copy(
            src_ref=send_delta.at[pl.ds(pl.multiple_of(p * 8, 8), 8)],
            dst_ref=recv_delta.at[mine],
            send_sem=delta_send_sem.at[k],
            recv_sem=delta_recv_sem.at[k],
            device_id=(p, tp),
            device_id_type=MESH,
        )
        copy.start()
        delta_copies.append(copy)
    recv_delta[mine, :] = send_delta[mine, :]

    zero = jnp.zeros((pairs, LANES), F32)
    total, blended = lax.fori_loop(0, tiles, weight_step, (zero, zero))
    total = jnp.sum(total, axis=1, keepdims=True)

    for copy in base_copies:
        copy.wait_recv()
    base = recv_base[0].astype(F32)
    for t in range(1, n_tp):
        base += recv_base[t].astype(F32)
    column = iota((rows, 8 * n_pool), 1)
    slot_of = (column // 8) * CAP + lax.rem(column, 8) // 2
    live = lax.rem(column, 8) < 2 * CAP
    picks = [
        (slot_of.astype(F32) == target) & live & (lax.rem(column, 2) == half) for half in range(2)
    ]
    pick = jnp.concatenate([jnp.where(m, 1.0, 0.0) for m in picks], axis=0).astype(BF16)
    for copy in delta_copies:
        copy.wait_recv()
    rows_delta = jnp.dot(pick, recv_delta[...].astype(BF16), preferred_element_type=F32)
    new_key = (base[:, :head] + rows_delta[:rows]).astype(BF16)
    new_value = (base[:, head:] + rows_delta[rows:]).astype(BF16)
    new_kv_ref[:, :head] = new_key
    new_kv_ref[:, head:] = new_value
    new_key, new_value = new_key.astype(F32)[None], new_value.astype(F32)[None]
    own = jnp.sum(
        (query.astype(F32).reshape(group, rows, head) * new_key).reshape(pairs, head), axis=1, keepdims=True
    ) * scale
    top = jnp.maximum(largest, own)
    fade = jnp.exp2(largest - top)
    own = jnp.exp2(own - top)
    total = total * fade + own
    rounded = own.astype(BF16).astype(F32)
    spread_own = jnp.broadcast_to(rounded, (pairs, head)).reshape(group, rows, head) * new_value
    result = (blended * fade + spread_own.reshape(pairs, head)) / total
    for h in range(group):
        attended_ref[:, h * head : (h + 1) * head] = result[h * rows : (h + 1) * rows].astype(BF16)

    for copy in row_copies + base_copies + rank_copies + delta_copies:
        copy.wait_send()


def body(
    dims,
    hidden,
    queries,
    key_value_weight,
    adapter_down_maps,
    adapter_up_maps,
    key_value_pages,
    row_adapter_index,
    adapter_page_position,
    row_page_table,
    cached_length,
):
    rows, feats = hidden.shape
    heads = key_value_weight.shape[1]
    width = key_value_weight.shape[2]
    adapters, _, double_rank = adapter_down_maps.shape
    n_pages, page = key_value_pages.shape[:2]
    n_pool = dims[0] * dims[1] * dims[2]
    positions = n_pages * page
    slots = CAP * n_pool
    span = CAP * feats // LANES
    pairs = rows * queries.shape[1] // LANES
    operands = (
        hidden,
        queries,
        key_value_weight.reshape(feats * heads, width),
        adapter_down_maps.reshape(adapters * feats, double_rank),
        adapter_up_maps.reshape(adapters * double_rank, width // 2),
        key_value_pages.reshape(positions, width),
        row_adapter_index.reshape(1, rows),
        adapter_page_position.reshape(1, -1),
        row_page_table.T,
        cached_length.reshape(1, rows),
    )
    vmem = [pltpu.VMEM(x.shape, x.dtype) for x in operands]
    scratch = vmem + [
        pltpu.VMEM((n_pool, 2 * span, LANES), BF16),
        pltpu.VMEM((n_pool, 2 * span, LANES), BF16),
        pltpu.VMEM((n_pool * span, LANES), F32),
        pltpu.VMEM((n_pool * span, LANES), F32),
        pltpu.VMEM((heads, rows, width), BF16),
        pltpu.VMEM((heads, rows, width), BF16),
        pltpu.VMEM((slots, LANES), BF16),
        pltpu.VMEM((heads, slots, LANES), BF16),
        pltpu.VMEM((n_pool * 8, LANES), F32),
        pltpu.VMEM((n_pool * 8, LANES), F32),
        pltpu.VMEM((rows, positions), F32),
        pltpu.VMEM((positions // 256, pairs, 256), F32),
        pltpu.SemaphoreType.DMA((len(operands),)),
        pltpu.SemaphoreType.DMA((n_pool - 1,)),
        pltpu.SemaphoreType.DMA((n_pool - 1,)),
        pltpu.SemaphoreType.DMA((heads - 1,)),
        pltpu.SemaphoreType.DMA((heads - 1,)),
        pltpu.SemaphoreType.DMA((heads - 1,)),
        pltpu.SemaphoreType.DMA((heads - 1,)),
        pltpu.SemaphoreType.DMA((n_pool - 1,)),
        pltpu.SemaphoreType.DMA((n_pool - 1,)),
    ]
    new_kv, attended = pl.pallas_call(
        functools.partial(kernel, dims, heads),
        out_shape=(
            jax.ShapeDtypeStruct((rows, width), BF16),
            jax.ShapeDtypeStruct(queries.shape, BF16),
        ),
        in_specs=[pl.BlockSpec(memory_space=pl.ANY)] * len(operands),
        out_specs=(pl.BlockSpec(memory_space=pltpu.VMEM),) * 2,
        scratch_shapes=scratch,
        compiler_params=pltpu.CompilerParams(
            collective_id=0, has_side_effects=True, vmem_limit_bytes=60 * 1024 * 1024
        ),
        name="decode_step",
    )(*operands)
    return new_kv.reshape(rows, 1, width), attended


def solution(mesh):
    placed = (
        P("pool", "tp"),
        P("pool", "tp"),
        P("tp", None, None),
        P("pool", "tp", None),
        P("pool", None, None, "tp", None),
        P("pool", None, "tp", None),
        P("pool"),
        P(),
        P("pool", None),
        P("pool"),
    )
    n_pool = mesh.shape["pool"]
    dims = (4, 4, 2) if n_pool == 32 else (1, n_pool // 2, 2)
    return jax.shard_map(
        functools.partial(body, dims),
        mesh=mesh,
        in_specs=placed,
        out_specs=(P("pool", "tp", None), P("pool", "tp")),
        check_vma=False,
    )
```

time: 318 us -> 34.6 us (0.11); the launches traced: 312 us -> 34.4 us
  waiting for transfers between devices: 196 us -> 0 us
  blocking collectives: 42.2 us -> 0 us
  Pallas kernels: 0 us -> 31 us
  starting transfers between devices: 22.1 us -> 0 us
  matrix products: 19.7 us -> 0 us
  between operations: 14.3 us -> 0.64 us
  local copies, waits for them, and re-layouts: 16.2 us -> 2.8 us
    all_to_all x2 -> x0, waiting for transfers between devices: 196 us -> none  [the longest x1 196 us: body(): lax.all_to_all(down_map_selected, 'pool', split_axis=0, concat_axis=0, ti...]
    pallas_call x0 -> x1, Pallas kernels: none -> 31 us  [body(): pl.pallas_call(functools.partial(kernel, dims, heads), out_shape=(jax.Sha...]
    psum x1 -> x0, blocking collectives: 26.9 us -> none  [body(): shrink = lax.psum(partial_rank, 'tp').astype(jnp.bfloat16)]
    all_to_all x2 -> x0, starting transfers between devices: 22.1 us -> none  [the longest x1 16.5 us: body(): lax.all_to_all(up_map_selected, 'pool', split_axis=0, concat_axis=0, tile...]
    dot_general x9 -> x0, matrix products: 19.7 us -> none  [the longest x1 7 us: body(): jnp.einsum('sd,sdk->sk', send_x, got_down.reshape(slot_total, feature_sha...]
    all_to_all x1 -> x0, blocking collectives: 15.3 us -> none  [body(): lax.all_to_all(send_local.reshape(pool_width, page_capacity), 'pool', spl...]
    gather x3 -> x0, local copies, waits for them, and re-layouts: 14.5 us -> none  [the longest x1 8.95 us: body(): adapter_down_maps[flat_requested]]
  transfers between devices with their start and end apart: 3 -> 0, of which waited for: 1 -> 0; matrix products, arithmetic and copies ran while one was open for 7% -> 0% of each run, Pallas kernels for 0% -> 0%
where the time goes in v1:
time: 34.6 us; the launch traced here: 34.4 us
  Pallas kernels  31 us (90%)
  local copies, waits for them, and re-layouts  2.8 us (8%)
  between operations  0.64 us (2%)
    pallas_call x1, Pallas kernels, body(): pl.pallas_call(functools.partial(kernel, dims, heads), out_shape=(jax.Sha...  31 us
    unnamed x2, local copies, waits for them, and re-layouts  2.8 us

profile of v1, /device:TPU:1, one launch (start us, length us, event | category | flops | bytes accessed | tf_op | source)
XLA Modules:
  0.0 34.4 jit_solution(1043900926447499453)
XLA Ops:
  0.6 31.0 %decode_step.1 = (bf16[32,256]{1,0:T(8,128)(2,1)}, bf16[32,1024]{1,0:T(8,128)(2,1)}) custom-call(bf16[32,1024]{1,0:T(8,128)(2,1)} %hid_hbm.1, bf16[32,1024]{1,0:T(8,128)(2,1)} %q_hbm.1, bf16[8192,256]{1,0:T(8,128)(2,1)} %bitcast.9, bf16[8192,128]{1,0:T(8,128)(2,1)} %bitcast.11, bf16[1024,128]{1,0:T(8,128)(2,1)} %bitcast.12, bf16[4352,256]{1,0:T(8,128)(2,1)} %bitcast.10, ...), custom_call_target="tpu_custom_call" | custom-call | tf_op jit(solution)/shard_map/decode_step/pallas_call | solution.py:439
  31.6 1.3 %copy.14 = bf16[32,1,256]{2,0,1:T(8,128)(2,1)} copy(bf16[32,1,256]{2,0,1:T(8,128)(2,1)} %bitcast.13) | data formatting | bytes 32768
  33.0 1.5 %copy.15 = bf16[32,1024]{1,0:T(8,128)(2,1)} copy(bf16[32,1024]{1,0:T(8,128)(2,1)} %get-tuple-element.9) | data formatting | bytes 131072

commit v2 on v1

--- a/solution.py
+++ b/solution.py
@@ -37,6 +37,10 @@
     x = lax.rem(lax.rem(me // nc, nx) + step[1], nx)
     c = lax.rem(lax.rem(me, nc) + step[2], nc)
     return (y * nx + x) * nc + c
+
+
+def wait_bytes(ref, sem):
+    pltpu.make_async_copy(ref, ref, sem).wait()
 
 
 def kernel(
@@ -66,25 +70,25 @@
     length,
     send_rows,
     recv_rows,
+    send_meta,
+    recv_meta,
     row_f32,
-    meta_f32,
     send_base,
     recv_base,
     send_rank,
     recv_rank,
+    up_mask,
+    delta_lines,
     send_delta,
     recv_delta,
     bias,
     scores,
     load_sem,
-    row_send_sem,
-    row_recv_sem,
-    base_send_sem,
-    base_recv_sem,
-    rank_send_sem,
-    rank_recv_sem,
-    delta_send_sem,
-    delta_recv_sem,
+    row_sems,
+    meta_sems,
+    base_sems,
+    rank_sems,
+    delta_sems,
 ):
     me = lax.axis_index("pool")
     tp = lax.axis_index("tp")
@@ -99,7 +103,8 @@
     span = CAP * chunks
     offsets = pool_offsets(dims)
     partners = [pool_partner(me, dims, s) for s in offsets]
-    tp_partners = [lax.rem(tp + s, n_tp) for s in range(1, n_tp)]
+    tp_steps = sorted(range(1, n_tp), key=lambda s: -ring(n_tp, s))
+    tp_partners = [lax.rem(tp + s, n_tp) for s in tp_steps]
 
     loads = [
         pltpu.make_async_copy(src, dst, load_sem.at[i])
@@ -119,14 +124,13 @@
         )
     ]
     (l_rai, l_app, l_hid, l_w, l_table, l_length, l_q, l_down, l_pages, l_up) = loads
+    barrier = pltpu.get_barrier_semaphore()
+    for t in tp_partners:
+        pl.semaphore_signal(barrier, inc=1, device_id=(me, t), device_id_type=MESH)
+    for p in partners:
+        pl.semaphore_signal(barrier, inc=1, device_id=(p, tp), device_id_type=MESH)
     for load in loads:
         load.start()
-
-    barrier = pltpu.get_barrier_semaphore()
-    for p in partners:
-        pl.semaphore_signal(barrier, inc=1, device_id=(p, tp), device_id_type=MESH)
-    for t in tp_partners:
-        pl.semaphore_signal(barrier, inc=1, device_id=(me, t), device_id_type=MESH)
 
     l_rai.wait()
     l_app.wait()
@@ -153,29 +157,37 @@
     place = jnp.where(place, 1.0, 0.0).astype(BF16)
     l_hid.wait()
     stacked = jnp.concatenate([hid[:, c * LANES : (c + 1) * LANES] for c in range(chunks)], axis=0)
-    local_lines = jnp.broadcast_to(local, (rows, LANES)).astype(BF16)
-    local_stack = jnp.concatenate([local_lines] * chunks, axis=0)
-    packets = jnp.dot(
-        place, jnp.concatenate([stacked, local_stack], axis=1), preferred_element_type=F32
+    packets = jnp.dot(place, stacked, preferred_element_type=F32).astype(BF16)
+    send_rows[...] = packets.reshape(n_pool, span, LANES)
+    first_half = iota((rows, LANES), 1) < LANES // 2
+    held_by = iota((n_pool, CAP * rows), 0) * CAP + iota((n_pool, CAP * rows), 1) // rows
+    held_by = jnp.where(held_by.astype(F32) == target_lane[:, : CAP * rows], 1.0, 0.0).astype(BF16)
+    lines = jnp.concatenate(
+        [jnp.where(first_half, local, 0.0), jnp.where(first_half, 0.0, local)], axis=0
     ).astype(BF16)
-    send_rows[:, 0:span, :] = packets[:, :LANES].reshape(n_pool, span, LANES)
-    send_rows[:, span : 2 * span, :] = packets[:, LANES:].reshape(n_pool, span, LANES)
+    send_meta[...] = jnp.dot(held_by, lines, preferred_element_type=F32).reshape(n_pool, 1, LANES)
 
     pl.semaphore_wait(barrier, len(partners) + len(tp_partners))
 
-    row_copies = []
-    for k, p in enumerate(partners):
-        copy = pltpu.make_async_remote_copy(
+    for p in partners:
+        pltpu.make_async_remote_copy(
             src_ref=send_rows.at[p],
             dst_ref=recv_rows.at[me],
-            send_sem=row_send_sem.at[k],
-            recv_sem=row_recv_sem.at[k],
+            send_sem=row_sems.at[0],
+            recv_sem=row_sems.at[1],
             device_id=(p, tp),
             device_id_type=MESH,
-        )
-        copy.start()
-        row_copies.append(copy)
+        ).start()
+        pltpu.make_async_remote_copy(
+            src_ref=send_meta.at[p],
+            dst_ref=recv_meta.at[me],
+            send_sem=meta_sems.at[0],
+            recv_sem=meta_sems.at[1],
+            device_id=(p, tp),
+            device_id_type=MESH,
+        ).start()
     recv_rows[me] = send_rows[me]
+    recv_meta[me] = send_meta[me]
 
     wide = LANES * heads
     spread = iota((LANES, wide), 0) == iota((LANES, wide), 1) // heads
@@ -191,25 +203,22 @@
         )
         base += jnp.dot(masked, w[c * wide : (c + 1) * wide, :], preferred_element_type=F32)
     send_base[...] = base.astype(BF16).reshape(heads, rows, 2 * head)
-    base_copies = []
-    for k, t in enumerate(tp_partners):
-        copy = pltpu.make_async_remote_copy(
+    for t in tp_partners:
+        pltpu.make_async_remote_copy(
             src_ref=send_base.at[t],
             dst_ref=recv_base.at[tp],
-            send_sem=base_send_sem.at[k],
-            recv_sem=base_recv_sem.at[k],
+            send_sem=base_sems.at[0],
+            recv_sem=base_sems.at[1],
             device_id=(me, t),
             device_id_type=MESH,
-        )
-        copy.start()
-        base_copies.append(copy)
+        ).start()
     recv_base[tp] = send_base[tp]
 
     l_down.wait()
-    for copy in row_copies:
-        copy.wait_recv()
-    row_f32[...] = recv_rows[:, 0:span, :].astype(F32).reshape(n_pool * span, LANES)
-    meta_f32[...] = recv_rows[:, span : 2 * span, :].astype(F32).reshape(n_pool * span, LANES)
+    others = pl.ds(0, n_pool - 1)
+    wait_bytes(recv_rows.at[others], row_sems.at[1])
+    wait_bytes(recv_meta.at[others], meta_sems.at[1])
+    row_f32[...] = recv_rows[...].astype(F32).reshape(n_pool * span, LANES)
     taken = jnp.concatenate(
         [
             jnp.concatenate(
@@ -219,26 +228,30 @@
         ],
         axis=0,
     ).astype(BF16)
+    meta = recv_meta[...].reshape(n_pool, LANES)
+    turned = pltpu.roll(meta, LANES // 2, 1)
+    first_half = iota((n_pool, LANES), 1) < LANES // 2
     adapter_of = jnp.concatenate(
-        [meta_f32[pl.ds(s * chunks, n_pool, stride=span), :] for s in range(CAP)], axis=0
+        [jnp.where(first_half, meta, turned), jnp.where(first_half, turned, meta)], axis=0
     )
     partial = jnp.zeros((slots, LANES), F32)
-    for a in range(adapters):
-        product = jnp.dot(taken, down[a * feats : (a + 1) * feats, :], preferred_element_type=F32)
-        partial = jnp.where(adapter_of == float(a), product, partial)
+    for a in range(0, adapters, 2):
+        both = jnp.concatenate(
+            [down[a * feats : (a + 1) * feats, :], down[(a + 1) * feats : (a + 2) * feats, :]], axis=1
+        )
+        product = jnp.dot(taken, both, preferred_element_type=F32)
+        partial = jnp.where(adapter_of == float(a), product[:, :LANES], partial)
+        partial = jnp.where(adapter_of == float(a + 1), product[:, LANES:], partial)
     send_rank[...] = partial.astype(BF16)
-    rank_copies = []
-    for k, t in enumerate(tp_partners):
-        copy = pltpu.make_async_remote_copy(
+    for t in tp_partners:
+        pltpu.make_async_remote_copy(
             src_ref=send_rank,
             dst_ref=recv_rank.at[tp],
-            send_sem=rank_send_sem.at[k],
-            recv_sem=rank_recv_sem.at[k],
+            send_sem=rank_sems.at[0],
+            recv_sem=rank_sems.at[1],
             device_id=(me, t),
             device_id_type=MESH,
-        )
-        copy.start()
-        rank_copies.append(copy)
+        ).start()
     recv_rank[tp] = send_rank[...]
 
     l_table.wait()
@@ -299,62 +312,56 @@
         )
         return total, blended
 
+    key_lane = iota((slots, LANES), 1) < LANES // 2
+    for half, lane in enumerate((key_lane, jnp.logical_not(key_lane))):
+        for a in range(adapters):
+            on = jnp.where((adapter_of == float(a)) & lane, 1.0, 0.0).astype(BF16)
+            up_mask[half * slots : (half + 1) * slots, a * LANES : (a + 1) * LANES] = on
     l_up.wait()
-    for copy in rank_copies:
-        copy.wait_recv()
+    wait_bytes(recv_rows.at[others], row_sems.at[0])
+    wait_bytes(recv_meta.at[others], meta_sems.at[0])
+    wait_bytes(recv_base.at[pl.ds(0, n_tp - 1)], base_sems.at[0])
+    wait_bytes(recv_rank.at[pl.ds(0, n_tp - 1)], rank_sems.at[1])
     shrink = recv_rank[0].astype(F32)
     for t in range(1, n_tp):
         shrink += recv_rank[t].astype(F32)
-    shrink = shrink.astype(BF16).astype(F32)
-    key_lane = iota((slots, LANES), 1) < LANES // 2
-    halves = [
-        jnp.concatenate(
-            [jnp.where((adapter_of == float(a)) & lane, shrink, 0.0) for a in range(adapters)], axis=1
-        )
-        for lane in (key_lane, jnp.logical_not(key_lane))
-    ]
-    delta = jnp.dot(jnp.concatenate(halves, axis=0).astype(BF16), up[...], preferred_element_type=F32)
+    shrink = shrink.astype(BF16)
+    spread_rank = jnp.concatenate([shrink] * adapters, axis=1)
+    spread_rank = jnp.concatenate([spread_rank] * 2, axis=0) * up_mask[...]
+    delta = jnp.dot(spread_rank, up[...], preferred_element_type=F32)
     delta = (delta * adapter_scale).astype(BF16).astype(F32)
     for s in range(CAP):
         for half in range(2):
             first = half * slots + s * n_pool
-            send_delta[pl.ds(s * 2 + half, n_pool, stride=8), :] = delta[first : first + n_pool, :]
-    for blank in range(2 * CAP, 8):
-        send_delta[pl.ds(blank, n_pool, stride=8), :] = jnp.zeros((n_pool, LANES), F32)
-    delta_copies = []
-    mine = pl.ds(pl.multiple_of(me * 8, 8), 8)
-    for k, p in enumerate(partners):
-        copy = pltpu.make_async_remote_copy(
-            src_ref=send_delta.at[pl.ds(pl.multiple_of(p * 8, 8), 8)],
-            dst_ref=recv_delta.at[mine],
-            send_sem=delta_send_sem.at[k],
-            recv_sem=delta_recv_sem.at[k],
+            delta_lines[pl.ds(s * 2 + half, n_pool, stride=2 * CAP), :] = delta[first : first + n_pool, :]
+    send_delta[...] = delta_lines[...].reshape(n_pool, 2 * CAP, LANES)
+    for p in partners:
+        pltpu.make_async_remote_copy(
+            src_ref=send_delta.at[p],
+            dst_ref=recv_delta.at[me],
+            send_sem=delta_sems.at[0],
+            recv_sem=delta_sems.at[1],
             device_id=(p, tp),
             device_id_type=MESH,
-        )
-        copy.start()
-        delta_copies.append(copy)
-    recv_delta[mine, :] = send_delta[mine, :]
+        ).start()
+    recv_delta[me] = send_delta[me]
 
     zero = jnp.zeros((pairs, LANES), F32)
     total, blended = lax.fori_loop(0, tiles, weight_step, (zero, zero))
     total = jnp.sum(total, axis=1, keepdims=True)
 
-    for copy in base_copies:
-        copy.wait_recv()
+    wait_bytes(recv_base.at[pl.ds(0, n_tp - 1)], base_sems.at[1])
     base = recv_base[0].astype(F32)
     for t in range(1, n_tp):
         base += recv_base[t].astype(F32)
-    column = iota((rows, 8 * n_pool), 1)
-    slot_of = (column // 8) * CAP + lax.rem(column, 8) // 2
-    live = lax.rem(column, 8) < 2 * CAP
-    picks = [
-        (slot_of.astype(F32) == target) & live & (lax.rem(column, 2) == half) for half in range(2)
-    ]
+    column = iota((rows, 2 * slots), 1)
+    mine = (column // 2).astype(F32) == target
+    picks = [mine & (lax.rem(column, 2) == half) for half in range(2)]
     pick = jnp.concatenate([jnp.where(m, 1.0, 0.0) for m in picks], axis=0).astype(BF16)
-    for copy in delta_copies:
-        copy.wait_recv()
-    rows_delta = jnp.dot(pick, recv_delta[...].astype(BF16), preferred_element_type=F32)
+    wait_bytes(recv_rank.at[pl.ds(0, n_tp - 1)], rank_sems.at[0])
+    wait_bytes(recv_delta.at[others], delta_sems.at[1])
+    arrived = recv_delta[...].reshape(2 * slots, LANES).astype(BF16)
+    rows_delta = jnp.dot(pick, arrived, preferred_element_type=F32)
     new_key = (base[:, :head] + rows_delta[:rows]).astype(BF16)
     new_value = (base[:, head:] + rows_delta[rows:]).astype(BF16)
     new_kv_ref[:, :head] = new_key
@@ -369,12 +376,11 @@
     total = total * fade + own
     rounded = own.astype(BF16).astype(F32)
     spread_own = jnp.broadcast_to(rounded, (pairs, head)).reshape(group, rows, head) * new_value
-    result = (blended * fade + spread_own.reshape(pairs, head)) / total
+    result = (blended * fade + spread_own.reshape(pairs, head)) * (1.0 / total)
     for h in range(group):
         attended_ref[:, h * head : (h + 1) * head] = result[h * rows : (h + 1) * rows].astype(BF16)
 
-    for copy in row_copies + base_copies + rank_copies + delta_copies:
-        copy.wait_send()
+    wait_bytes(recv_delta.at[others], delta_sems.at[0])
 
 
 def body(
@@ -414,33 +420,29 @@
     )
     vmem = [pltpu.VMEM(x.shape, x.dtype) for x in operands]
     scratch = vmem + [
-        pltpu.VMEM((n_pool, 2 * span, LANES), BF16),
-        pltpu.VMEM((n_pool, 2 * span, LANES), BF16),
-        pltpu.VMEM((n_pool * span, LANES), F32),
+        pltpu.VMEM((n_pool, span, LANES), BF16),
+        pltpu.VMEM((n_pool, span, LANES), BF16),
+        pltpu.VMEM((n_pool, 1, LANES), F32),
+        pltpu.VMEM((n_pool, 1, LANES), F32),
         pltpu.VMEM((n_pool * span, LANES), F32),
         pltpu.VMEM((heads, rows, width), BF16),
         pltpu.VMEM((heads, rows, width), BF16),
         pltpu.VMEM((slots, LANES), BF16),
         pltpu.VMEM((heads, slots, LANES), BF16),
-        pltpu.VMEM((n_pool * 8, LANES), F32),
-        pltpu.VMEM((n_pool * 8, LANES), F32),
+        pltpu.VMEM((2 * slots, adapters * LANES), BF16),
+        pltpu.VMEM((2 * slots, LANES), F32),
+        pltpu.VMEM((n_pool, 2 * CAP, LANES), F32),
+        pltpu.VMEM((n_pool, 2 * CAP, LANES), F32),
         pltpu.VMEM((rows, positions), F32),
         pltpu.VMEM((positions // 256, pairs, 256), F32),
         pltpu.SemaphoreType.DMA((len(operands),)),
-        pltpu.SemaphoreType.DMA((n_pool - 1,)),
-        pltpu.SemaphoreType.DMA((n_pool - 1,)),
-        pltpu.SemaphoreType.DMA((heads - 1,)),
-        pltpu.SemaphoreType.DMA((heads - 1,)),
-        pltpu.SemaphoreType.DMA((heads - 1,)),
-        pltpu.SemaphoreType.DMA((heads - 1,)),
-        pltpu.SemaphoreType.DMA((n_pool - 1,)),
-        pltpu.SemaphoreType.DMA((n_pool - 1,)),
+        *[pltpu.SemaphoreType.DMA((2,)) for _ in range(5)],
     ]
     new_kv, attended = pl.pallas_call(
         functools.partial(kernel, dims, heads),
         out_shape=(
-            jax.ShapeDtypeStruct((rows, width), BF16),
-            jax.ShapeDtypeStruct(queries.shape, BF16),
+            pltpu.VMEM((rows, width), BF16),
+            pltpu.VMEM(queries.shape, BF16),
         ),
         in_specs=[pl.BlockSpec(memory_space=pl.ANY)] * len(operands),
         out_specs=(pl.BlockSpec(memory_space=pltpu.VMEM),) * 2,

time: 34.6 us -> 29.2 us (0.84)
  Pallas kernels: 31 us -> 27.3 us
  local copies, waits for them, and re-layouts: 2.8 us -> 1.24 us
    pallas_call x1, Pallas kernels: 31 us -> 27.3 us  [body(): pl.pallas_call(functools.partial(kernel, dims, heads), out_shape=(pltpu.V...]
    unnamed x2, local copies, waits for them, and re-layouts: 2.8 us -> 1.24 us
where the time goes in v2:
time: 29.2 us
  Pallas kernels  27.3 us (93%)
  local copies, waits for them, and re-layouts  1.24 us (4%)
  between operations  0.64 us (2%)
    pallas_call x1, Pallas kernels, body(): pl.pallas_call(functools.partial(kernel, dims, heads), out_shape=(pltpu.V...  27.3 us
    unnamed x2, local copies, waits for them, and re-layouts  1.24 us

profile of v2, /device:TPU:1, one launch (start us, length us, event | category | flops | bytes accessed | tf_op | source)
XLA Modules:
  0.0 29.2 jit_solution(7721767632855278866)
XLA Ops:
  0.6 27.3 %decode_step.1 = (bf16[32,256]{1,0:T(8,128)(2,1)S(1)}, bf16[32,1024]{1,0:T(8,128)(2,1)S(1)}) custom-call(bf16[32,1024]{1,0:T(8,128)(2,1)} %hid_hbm.1, bf16[32,1024]{1,0:T(8,128)(2,1)} %q_hbm.1, bf16[8192,256]{1,0:T(8,128)(2,1)} %bitcast.10, bf16[8192,128]{1,0:T(8,128)(2,1)} %bitcast.12, bf16[1024,128]{1,0:T(8,128)(2,1)} %bitcast.13, ...), custom_call_target="tpu_custom_call" | custom-call | tf_op jit(solution)/shard_map/decode_step/pallas_call | solution.py:441
  27.9 0.6 %copy.14 = bf16[32,1,256]{2,0,1:T(8,128)(2,1)} copy(bf16[32,1,256]{2,0,1:T(8,128)(2,1)S(1)} %bitcast.9) | data formatting | bytes 32768
  28.5 0.6 %copy.15 = bf16[32,1024]{1,0:T(8,128)(2,1)} copy(bf16[32,1024]{1,0:T(8,128)(2,1)S(1)} %get-tuple-element.7) | data formatting | bytes 131072

commit v3 on v2

--- a/solution.py
+++ b/solution.py
@@ -78,7 +78,6 @@
     send_rank,
     recv_rank,
     up_mask,
-    delta_lines,
     send_delta,
     recv_delta,
     bias,
@@ -89,6 +88,7 @@
     base_sems,
     rank_sems,
     delta_sems,
+    up_sems,
 ):
     me = lax.axis_index("pool")
     tp = lax.axis_index("tp")
@@ -103,6 +103,12 @@
     span = CAP * chunks
     offsets = pool_offsets(dims)
     partners = [pool_partner(me, dims, s) for s in offsets]
+    core = lax.rem(me, 2)
+    chip = me // 2
+    other_core = me + 1 - 2 * core
+    gather = me + 1 - core
+    n_chips = n_pool // 2
+    chip_slots = 2 * CAP
     tp_steps = sorted(range(1, n_tp), key=lambda s: -ring(n_tp, s))
     tp_partners = [lax.rem(tp + s, n_tp) for s in tp_steps]
 
@@ -119,7 +125,7 @@
                 (q_hbm, q),
                 (down_hbm, down),
                 (pages_hbm, pages),
-                (up_hbm, up),
+                (up_hbm, up.at[pl.ds(adapters * LANES, adapters * LANES)]),
             )
         )
     ]
@@ -127,6 +133,7 @@
     barrier = pltpu.get_barrier_semaphore()
     for t in tp_partners:
         pl.semaphore_signal(barrier, inc=1, device_id=(me, t), device_id_type=MESH)
+        pl.semaphore_signal(barrier, inc=1, device_id=(other_core, t), device_id_type=MESH)
     for p in partners:
         pl.semaphore_signal(barrier, inc=1, device_id=(p, tp), device_id_type=MESH)
     for load in loads:
@@ -159,15 +166,16 @@
     stacked = jnp.concatenate([hid[:, c * LANES : (c + 1) * LANES] for c in range(chunks)], axis=0)
     packets = jnp.dot(place, stacked, preferred_element_type=F32).astype(BF16)
     send_rows[...] = packets.reshape(n_pool, span, LANES)
-    first_half = iota((rows, LANES), 1) < LANES // 2
-    held_by = iota((n_pool, CAP * rows), 0) * CAP + iota((n_pool, CAP * rows), 1) // rows
-    held_by = jnp.where(held_by.astype(F32) == target_lane[:, : CAP * rows], 1.0, 0.0).astype(BF16)
-    lines = jnp.concatenate(
-        [jnp.where(first_half, local, 0.0), jnp.where(first_half, 0.0, local)], axis=0
-    ).astype(BF16)
-    send_meta[...] = jnp.dot(held_by, lines, preferred_element_type=F32).reshape(n_pool, 1, LANES)
-
-    pl.semaphore_wait(barrier, len(partners) + len(tp_partners))
+    wide_rows = chip_slots * rows
+    held_by = iota((n_chips, wide_rows), 0) * chip_slots + iota((n_chips, wide_rows), 1) // rows
+    held_by = jnp.where(held_by.astype(F32) == target_lane[:, :wide_rows], 1.0, 0.0).astype(BF16)
+    quarter = iota((rows, LANES), 1) // (LANES // chip_slots)
+    lines = jnp.concatenate([jnp.where(quarter == n, local, 0.0) for n in range(chip_slots)], axis=0)
+    send_meta[...] = jnp.dot(
+        held_by, lines.astype(BF16), preferred_element_type=F32
+    ).reshape(n_chips, 1, LANES)
+
+    pl.semaphore_wait(barrier, len(partners) + 2 * len(tp_partners))
 
     for p in partners:
         pltpu.make_async_remote_copy(
@@ -179,7 +187,7 @@
             device_id_type=MESH,
         ).start()
         pltpu.make_async_remote_copy(
-            src_ref=send_meta.at[p],
+            src_ref=send_meta.at[p // 2],
             dst_ref=recv_meta.at[me],
             send_sem=meta_sems.at[0],
             recv_sem=meta_sems.at[1],
@@ -187,7 +195,20 @@
             device_id_type=MESH,
         ).start()
     recv_rows[me] = send_rows[me]
-    recv_meta[me] = send_meta[me]
+    recv_meta[me] = send_meta[chip]
+    up_half = adapters * LANES
+    up_copy = pltpu.make_async_remote_copy(
+        src_ref=up_hbm,
+        dst_ref=up.at[pl.ds(0, up_half)],
+        send_sem=up_sems.at[0],
+        recv_sem=up_sems.at[1],
+        device_id=(other_core, tp),
+        device_id_type=MESH,
+    )
+
+    @pl.when(core == 0)
+    def _():
+        up_copy.start()
 
     wide = LANES * heads
     spread = iota((LANES, wide), 0) == iota((LANES, wide), 1) // heads
@@ -228,12 +249,18 @@
         ],
         axis=0,
     ).astype(BF16)
-    meta = recv_meta[...].reshape(n_pool, LANES)
-    turned = pltpu.roll(meta, LANES // 2, 1)
-    first_half = iota((n_pool, LANES), 1) < LANES // 2
-    adapter_of = jnp.concatenate(
-        [jnp.where(first_half, meta, turned), jnp.where(first_half, turned, meta)], axis=0
-    )
+    meta = recv_meta[...].reshape(n_pool, LANES).astype(BF16)
+    apart = iota((LANES, chip_slots * LANES), 1) // LANES * (LANES // chip_slots)
+    apart = jnp.where(iota((LANES, chip_slots * LANES), 0) == apart, 1.0, 0.0).astype(BF16)
+    spread_meta = jnp.dot(meta, apart, preferred_element_type=F32)
+    adapters_of = [
+        jnp.concatenate(
+            [spread_meta[:, (n * CAP + m) * LANES : (n * CAP + m + 1) * LANES] for m in range(CAP)], axis=0
+        )
+        for n in range(2)
+    ]
+    is_one = core.astype(F32)
+    adapter_of = adapters_of[0] * (1.0 - is_one) + adapters_of[1] * is_one
     partial = jnp.zeros((slots, LANES), F32)
     for a in range(0, adapters, 2):
         both = jnp.concatenate(
@@ -243,16 +270,27 @@
         partial = jnp.where(adapter_of == float(a), product[:, :LANES], partial)
         partial = jnp.where(adapter_of == float(a + 1), product[:, LANES:], partial)
     send_rank[...] = partial.astype(BF16)
-    for t in tp_partners:
+    rank_copies = [
         pltpu.make_async_remote_copy(
             src_ref=send_rank,
-            dst_ref=recv_rank.at[tp],
+            dst_ref=recv_rank.at[core * n_tp + tp],
             send_sem=rank_sems.at[0],
-            recv_sem=rank_sems.at[1],
-            device_id=(me, t),
+            recv_sem=rank_sems.at[1 + core],
+            device_id=(gather, t),
             device_id_type=MESH,
-        ).start()
-    recv_rank[tp] = send_rank[...]
+        )
+        for t in [*tp_partners, tp]
+    ]
+    for copy in rank_copies[:-1]:
+        copy.start()
+
+    @pl.when(core == 0)
+    def _():
+        rank_copies[-1].start()
+
+    @pl.when(core == 1)
+    def _():
+        recv_rank[n_tp + tp] = send_rank[...]
 
     l_table.wait()
     l_length.wait()
@@ -312,39 +350,75 @@
         )
         return total, blended
 
-    key_lane = iota((slots, LANES), 1) < LANES // 2
-    for half, lane in enumerate((key_lane, jnp.logical_not(key_lane))):
-        for a in range(adapters):
-            on = jnp.where((adapter_of == float(a)) & lane, 1.0, 0.0).astype(BF16)
-            up_mask[half * slots : (half + 1) * slots, a * LANES : (a + 1) * LANES] = on
-    l_up.wait()
     wait_bytes(recv_rows.at[others], row_sems.at[0])
     wait_bytes(recv_meta.at[others], meta_sems.at[0])
     wait_bytes(recv_base.at[pl.ds(0, n_tp - 1)], base_sems.at[0])
-    wait_bytes(recv_rank.at[pl.ds(0, n_tp - 1)], rank_sems.at[1])
-    shrink = recv_rank[0].astype(F32)
-    for t in range(1, n_tp):
-        shrink += recv_rank[t].astype(F32)
-    shrink = shrink.astype(BF16)
-    spread_rank = jnp.concatenate([shrink] * adapters, axis=1)
-    spread_rank = jnp.concatenate([spread_rank] * 2, axis=0) * up_mask[...]
-    delta = jnp.dot(spread_rank, up[...], preferred_element_type=F32)
-    delta = (delta * adapter_scale).astype(BF16).astype(F32)
-    for s in range(CAP):
-        for half in range(2):
-            first = half * slots + s * n_pool
-            delta_lines[pl.ds(s * 2 + half, n_pool, stride=2 * CAP), :] = delta[first : first + n_pool, :]
-    send_delta[...] = delta_lines[...].reshape(n_pool, 2 * CAP, LANES)
-    for p in partners:
-        pltpu.make_async_remote_copy(
-            src_ref=send_delta.at[p],
-            dst_ref=recv_delta.at[me],
-            send_sem=delta_sems.at[0],
-            recv_sem=delta_sems.at[1],
-            device_id=(p, tp),
-            device_id_type=MESH,
-        ).start()
-    recv_delta[me] = send_delta[me]
+    l_up.wait()
+
+    @pl.when(core == 1)
+    def _():
+        key_lane = iota((slots, LANES), 1) < LANES // 2
+        rank_width = LANES // 2
+        for n in range(2):
+            for a in range(0, adapters, 2):
+                on = jnp.where(key_lane, adapters_of[n], adapters_of[n] - 1.0) == float(a)
+                up_mask[n * slots : (n + 1) * slots, a * rank_width : (a + 2) * rank_width] = jnp.where(
+                    on, 1.0, 0.0
+                ).astype(BF16)
+        wait_bytes(up.at[pl.ds(0, up_half)], up_sems.at[1])
+        for n in (1, 0):
+            first = n * n_tp
+            wait_bytes(recv_rank.at[pl.ds(first, n_tp - n)], rank_sems.at[1 + n])
+            shrink = recv_rank[first].astype(F32)
+            for t in range(1, n_tp):
+                shrink += recv_rank[first + t].astype(F32)
+            shrink = shrink.astype(BF16).astype(F32)
+            swapped = pltpu.roll(shrink, rank_width, 1)
+            mask = up_mask[n * slots : (n + 1) * slots, :]
+            spread_rank = jnp.concatenate(
+                [
+                    jnp.concatenate([twice.astype(BF16)] * (adapters // 2), axis=1) * mask
+                    for twice in (
+                        jnp.where(key_lane, shrink, swapped),
+                        jnp.where(key_lane, swapped, shrink),
+                    )
+                ],
+                axis=0,
+            )
+            maps = jnp.concatenate(
+                [
+                    jnp.concatenate(
+                        [
+                            up[pl.ds(n * up_half + a * LANES + half * rank_width, rank_width), :]
+                            for a in range(adapters)
+                        ],
+                        axis=0,
+                    )
+                    for half in range(2)
+                ],
+                axis=1,
+            )
+            both = jnp.dot(spread_rank, maps, preferred_element_type=F32)
+            for half in range(2):
+                delta = both[half * slots : (half + 1) * slots, half * LANES : (half + 1) * LANES]
+                delta = (delta * adapter_scale).astype(BF16).astype(F32)
+                for m in range(CAP):
+                    line = (n * CAP + m) * 2 + half
+                    send_delta[pl.ds(line, n_pool, stride=2 * chip_slots), :] = delta[
+                        m * n_pool : (m + 1) * n_pool, :
+                    ]
+        packet = 2 * chip_slots
+        here = pl.ds(pl.multiple_of(chip * packet, packet), packet)
+        for p in partners:
+            pltpu.make_async_remote_copy(
+                src_ref=send_delta.at[pl.ds(pl.multiple_of(p * packet, packet), packet)],
+                dst_ref=recv_delta.at[here],
+                send_sem=delta_sems.at[0],
+                recv_sem=delta_sems.at[1],
+                device_id=(p, tp),
+                device_id_type=MESH,
+            ).start()
+        recv_delta[here, :] = send_delta[pl.ds(pl.multiple_of(me * packet, packet), packet), :]
 
     zero = jnp.zeros((pairs, LANES), F32)
     total, blended = lax.fori_loop(0, tiles, weight_step, (zero, zero))
@@ -358,9 +432,20 @@
     mine = (column // 2).astype(F32) == target
     picks = [mine & (lax.rem(column, 2) == half) for half in range(2)]
     pick = jnp.concatenate([jnp.where(m, 1.0, 0.0) for m in picks], axis=0).astype(BF16)
-    wait_bytes(recv_rank.at[pl.ds(0, n_tp - 1)], rank_sems.at[0])
-    wait_bytes(recv_delta.at[others], delta_sems.at[1])
-    arrived = recv_delta[...].reshape(2 * slots, LANES).astype(BF16)
+    packet = 2 * chip_slots
+
+    @pl.when(core == 0)
+    def _():
+        wait_bytes(up.at[pl.ds(0, up_half)], up_sems.at[0])
+        wait_bytes(recv_rank.at[pl.ds(0, n_tp)], rank_sems.at[0])
+        wait_bytes(recv_delta, delta_sems.at[1])
+
+    @pl.when(core == 1)
+    def _():
+        wait_bytes(recv_rank.at[pl.ds(0, n_tp - 1)], rank_sems.at[0])
+        wait_bytes(recv_delta.at[pl.ds(0, (n_chips - 1) * packet)], delta_sems.at[1])
+
+    arrived = recv_delta[...].astype(BF16)
     rows_delta = jnp.dot(pick, arrived, preferred_element_type=F32)
     new_key = (base[:, :head] + rows_delta[:rows]).astype(BF16)
     new_value = (base[:, head:] + rows_delta[rows:]).astype(BF16)
@@ -380,7 +465,20 @@
     for h in range(group):
         attended_ref[:, h * head : (h + 1) * head] = result[h * rows : (h + 1) * rows].astype(BF16)
 
-    wait_bytes(recv_delta.at[others], delta_sems.at[0])
+    @pl.when(core == 1)
+    def _():
+        wait_bytes(send_delta.at[pl.ds(0, (n_pool - 1) * packet)], delta_sems.at[0])
+
+
+def emit(new_kv_in, attended_in, new_kv_out, attended_out, sem):
+    copies = [
+        pltpu.make_async_copy(attended_in, attended_out, sem.at[0]),
+        pltpu.make_async_copy(new_kv_in, new_kv_out, sem.at[1]),
+    ]
+    for copy in copies:
+        copy.start()
+    for copy in copies:
+        copy.wait()
 
 
 def body(
@@ -419,24 +517,24 @@
         cached_length.reshape(1, rows),
     )
     vmem = [pltpu.VMEM(x.shape, x.dtype) for x in operands]
+    vmem[4] = pltpu.VMEM((2 * adapters * double_rank, width // 2), BF16)
     scratch = vmem + [
         pltpu.VMEM((n_pool, span, LANES), BF16),
         pltpu.VMEM((n_pool, span, LANES), BF16),
-        pltpu.VMEM((n_pool, 1, LANES), F32),
+        pltpu.VMEM((n_pool // 2, 1, LANES), F32),
         pltpu.VMEM((n_pool, 1, LANES), F32),
         pltpu.VMEM((n_pool * span, LANES), F32),
         pltpu.VMEM((heads, rows, width), BF16),
         pltpu.VMEM((heads, rows, width), BF16),
         pltpu.VMEM((slots, LANES), BF16),
-        pltpu.VMEM((heads, slots, LANES), BF16),
-        pltpu.VMEM((2 * slots, adapters * LANES), BF16),
+        pltpu.VMEM((2 * heads, slots, LANES), BF16),
+        pltpu.VMEM((2 * slots, adapters * LANES // 2), BF16),
+        pltpu.VMEM((4 * slots, LANES), F32),
         pltpu.VMEM((2 * slots, LANES), F32),
-        pltpu.VMEM((n_pool, 2 * CAP, LANES), F32),
-        pltpu.VMEM((n_pool, 2 * CAP, LANES), F32),
         pltpu.VMEM((rows, positions), F32),
         pltpu.VMEM((positions // 256, pairs, 256), F32),
         pltpu.SemaphoreType.DMA((len(operands),)),
-        *[pltpu.SemaphoreType.DMA((2,)) for _ in range(5)],
+        *[pltpu.SemaphoreType.DMA((3,)) for _ in range(6)],
     ]
     new_kv, attended = pl.pallas_call(
         functools.partial(kernel, dims, heads),
@@ -452,6 +550,18 @@
         ),
         name="decode_step",
     )(*operands)
+    new_kv, attended = pl.pallas_call(
+        emit,
+        out_shape=(
+            jax.ShapeDtypeStruct(new_kv.shape, BF16),
+            jax.ShapeDtypeStruct(attended.shape, BF16),
+        ),
+        in_specs=[pl.BlockSpec(memory_space=pl.ANY)] * 2,
+        out_specs=(pl.BlockSpec(memory_space=pl.ANY),) * 2,
+        scratch_shapes=[pltpu.SemaphoreType.DMA((2,))],
+        compiler_params=pltpu.CompilerParams(vmem_limit_bytes=1024 * 1024),
+        name="emit",
+    )(new_kv, attended)
     return new_kv.reshape(rows, 1, width), attended
 
 

time: 29.2 us -> 28.6 us (0.979)
  local copies, waits for them, and re-layouts: 1.24 us -> 0 us
  Pallas kernels: 27.3 us -> 27.9 us
    unnamed x2 -> x0, local copies, waits for them, and re-layouts: 1.24 us -> none
    pallas_call x0 -> x1, Pallas kernels: none -> 0.65 us  [body(): pl.pallas_call(emit, out_shape=(jax.ShapeDtypeStruct(new_kv.shape, BF16),...]
where the time goes in v3:
time: 28.6 us; the launch traced here: 28.5 us
  Pallas kernels  27.9 us (98%)
  between operations  0.64 us (2%)
    pallas_call x1, Pallas kernels, body(): pl.pallas_call(functools.partial(kernel, dims, heads), out_shape=(pltpu.V...  27.2 us
    pallas_call x1, Pallas kernels, body(): pl.pallas_call(emit, out_shape=(jax.ShapeDtypeStruct(new_kv.shape, BF16),...  0.65 us

profile of v3, /device:TPU:1, one launch (start us, length us, event | category | flops | bytes accessed | tf_op | source)
XLA Modules:
  0.0 28.5 jit_solution(13840488407580175835)
XLA Ops:
  0.6 27.2 %decode_step.1 = (bf16[32,256]{1,0:T(8,128)(2,1)S(1)}, bf16[32,1024]{1,0:T(8,128)(2,1)S(1)}) custom-call(bf16[32,1024]{1,0:T(8,128)(2,1)} %hid_hbm.1, bf16[32,1024]{1,0:T(8,128)(2,1)} %q_hbm.1, bf16[8192,256]{1,0:T(8,128)(2,1)} %bitcast.9, bf16[8192,128]{1,0:T(8,128)(2,1)} %bitcast.11, bf16[1024,128]{1,0:T(8,128)(2,1)} %bitcast.12, ...), custom_call_target="tpu_custom_call" | custom-call | tf_op jit(solution)/shard_map/decode_step/pallas_call | solution.py:539
  27.9 0.7 %emit.1 = (bf16[32,256]{1,0:T(8,128)(2,1)}, bf16[32,1024]{1,0:T(8,128)(2,1)}) custom-call(bf16[32,256]{1,0:T(8,128)(2,1)S(1)} %get-tuple-element.6.new_kv_in, bf16[32,1024]{1,0:T(8,128)(2,1)S(1)} %get-tuple-element.7.attended_in), custom_call_target="tpu_custom_call" | custom-call | tf_op jit(solution)/shard_map/emit/pallas_call | solution.py:553
